TPU v7x, 32 devices: a whole 2x2x4 slice. The times are simulated.
32 devices in a mesh: req: 8 (over z, x), head: 4 (over y, core).
Axes of the slice: x: 2, y: 2, z: 4, core: 2. Of those that a mesh axis runs over, the one named last changes fastest.
Arguments:
- residual: bfloat16 [128, 4096], P(None, 'req'), may hold values from -80 to 80
- lengths: int32 [128], P('req'), may hold values from 0 to 32768, as said below
- ssm_state: float32 [128, 128, 64, 128], P('req', 'head'), may hold values from -6 to 6
- tail_mix: float32 [128, 3, 8192], P('req', None, 'head'), may hold values from -6 to 6
- tail_group: float32 [128, 3, 2, 1024], P('req', None, None, 'head'), may hold values from -6 to 6
- norm_first: float32 [4096], P('req'), may hold values from 0.1 to 1.9
- mix_weight: bfloat16 [4096, 2, 8192], P('req', None, 'head'), may hold values from -0.09375 to 0.09375
- group_weight: bfloat16 [4096, 2, 1024], P('req', None, 'head'), may hold values from -0.09375 to 0.09375
- step_weight: bfloat16 [4096, 128], P('req', 'head'), may hold values from -0.09375 to 0.09375
- conv_mix: float32 [4, 8192], P(None, 'head'), may hold values from -3 to 3
- conv_group: float32 [4, 2, 1024], P(None, None, 'head'), may hold values from -3 to 3
- bias_mix: float32 [8192], P('head'), may hold values from -3 to 3
- bias_group: float32 [2, 1024], P(None, 'head'), may hold values from -3 to 3
- step_bias: float32 [128], P('head'), may hold values from -2 to 1
- decay_log: float32 [128], P('head'), may hold values from -1 to 2
- skip_gain: float32 [128], P('head'), may hold values from 0.5 to 2
- gate_gain: float32 [8192], P('head'), may hold values from 0.1 to 1.9
- out_weight: bfloat16 [8192, 4096], P('head', 'req'), may hold values from -0.0625 to 0.0625
- norm_second: float32 [4096], P('req'), may hold values from 0.1 to 1.9
- up_weight: bfloat16 [4096, 21504], P('req', 'head'), may hold values from -0.09375 to 0.09375
- down_weight: bfloat16 [21504, 4096], P('head', 'req'), may hold values from -0.0390625 to 0.0390625
Outputs:
- residual_out: bfloat16 [128, 4096], P(None, 'req')
- state_out: float32 [128, 128, 64, 128], P('req', 'head')
- tail_mix_out: float32 [128, 3, 8192], P('req', None, 'head')
- tail_group_out: float32 [128, 3, 2, 1024], P('req', None, None, 'head')
Inputs may be any that keep to these rules, and one draw needn't show every extreme that they name: `lengths`: 0 marks a fresh request.
All inputs are finite; a program needn't handle non-finite values.
Results may differ from a plain program's by a relative error of at most 0.0056.
Values may be sent and summed in bfloat16 or wider, within the bound.
A program may use at most 128 MiB of HBM per device.

v0:
```python
import jax
import jax.numpy as jnp
from jax import lax
from jax.sharding import PartitionSpec as P

eps = 1e-05


def square_sums(values):
    wide = values.astype(jnp.float32)
    return jnp.sum(wide * wide, axis=1)


def norm_total(partial_sum):
    return lax.psum(partial_sum, "req")


def inverse_of(total, count):
    return lax.rsqrt(total / count + eps)


def head_total(partial_sum):
    return lax.psum(partial_sum, "head")


def on_device(
    residual,
    lengths,
    ssm_state,
    tail_mix,
    tail_group,
    norm_first,
    mix_weight,
    group_weight,
    step_weight,
    conv_mix,
    conv_group,
    bias_mix,
    bias_group,
    step_bias,
    decay_log,
    skip_gain,
    gate_gain,
    out_weight,
    norm_second,
    up_weight,
    down_weight,
):
    rows_dev = ssm_state.shape[0]
    heads_dev = ssm_state.shape[1]
    head_dim = ssm_state.shape[2]
    state_size = ssm_state.shape[3]
    mix_dev = mix_weight.shape[2]
    group_dev = group_weight.shape[2]
    groups_dev = group_dev // state_size
    per_group = heads_dev // groups_dev
    width_dev = residual.shape[1]
    width_all = width_dev * lax.axis_size("req")
    taps_all = conv_mix.shape[0]
    first_row = lax.axis_index("req") * rows_dev
    partial_one = square_sums(residual)
    scaled = (residual.astype(jnp.float32) * norm_first).astype(jnp.bfloat16)
    mix_flat = mix_weight.reshape(width_dev, 2 * mix_dev)
    group_flat = group_weight.reshape(width_dev, 2 * group_dev)
    pieces = [
        jnp.dot(scaled, mix_flat, preferred_element_type=jnp.float32),
        jnp.dot(scaled, group_flat, preferred_element_type=jnp.float32),
        jnp.dot(scaled, step_weight, preferred_element_type=jnp.float32),
    ]
    sums = lax.psum_scatter(jnp.concatenate(pieces, axis=1), "req", scatter_dimension=0, tiled=True)
    total_one = lax.dynamic_slice_in_dim(norm_total(partial_one), first_row, rows_dev, 0)
    sums = sums * inverse_of(total_one, width_all)[:, None]
    gate_z = sums[:, :mix_dev]
    mix_in = sums[:, mix_dev : 2 * mix_dev]
    group_in = sums[:, 2 * mix_dev : 2 * mix_dev + 2 * group_dev].reshape(rows_dev, 2, group_dev)
    step_raw = sums[:, 2 * mix_dev + 2 * group_dev :]
    valid = jnp.minimum(lengths, taps_all - 1)
    slots = jnp.arange(taps_all - 1)
    keep = (slots[None, :] >= (taps_all - 1 - valid)[:, None]).astype(jnp.float32)
    window_mix = jnp.concatenate([tail_mix * keep[:, :, None], mix_in[:, None, :]], axis=1)
    window_group = jnp.concatenate([tail_group * keep[:, :, None, None], group_in[:, None]], axis=1)
    conv_x = jax.nn.silu(jnp.sum(window_mix * conv_mix[None], axis=1) + bias_mix)
    conv_bc = jax.nn.silu(jnp.sum(window_group * conv_group[None], axis=1) + bias_group)
    step_size = jax.nn.softplus(step_raw + step_bias)
    alive = (lengths > 0).astype(jnp.float32)
    decay = jnp.exp(-step_size * jnp.exp(decay_log)) * alive[:, None]
    inputs = conv_x.reshape(rows_dev, groups_dev, per_group, head_dim)
    b_vector = conv_bc[:, 0].reshape(rows_dev, groups_dev, 1, 1, state_size)
    c_vector = conv_bc[:, 1].reshape(rows_dev, groups_dev, state_size)
    prior = ssm_state.reshape(rows_dev, groups_dev, per_group, head_dim, state_size)
    rate = decay.reshape(rows_dev, groups_dev, per_group, 1, 1)
    stride = step_size.reshape(rows_dev, groups_dev, per_group, 1)
    updated = rate * prior + (stride * inputs)[..., None] * b_vector
    readout = jnp.einsum("rgepn,rgn->rgep", updated, c_vector, precision=lax.Precision.HIGHEST)
    readout = readout + skip_gain.reshape(1, groups_dev, per_group, 1) * inputs
    mixed = readout.reshape(rows_dev, mix_dev)
    state_out = updated.reshape(ssm_state.shape)
    gated = mixed * jax.nn.silu(gate_z)
    grouped = gated.reshape(rows_dev, groups_dev, -1)
    inverse = lax.rsqrt(jnp.mean(grouped * grouped, axis=2, keepdims=True) + eps)
    normed_y = ((grouped * inverse).reshape(rows_dev, mix_dev) * gate_gain).astype(jnp.bfloat16)
    mixer = head_total(
        jnp.dot(
            lax.all_gather(normed_y, "req", axis=0, tiled=True),
            out_weight,
            preferred_element_type=jnp.float32,
        )
    )
    middle = (residual.astype(jnp.float32) + mixer).astype(jnp.bfloat16)
    partial_two = square_sums(middle)
    scaled_two = (middle.astype(jnp.float32) * norm_second).astype(jnp.bfloat16)
    activation = jnp.dot(scaled_two, up_weight, preferred_element_type=jnp.float32)
    total_two = norm_total(partial_two)
    share = lax.psum_scatter(activation, "req", scatter_dimension=1, tiled=True)
    share = share * inverse_of(total_two, width_all)[:, None]
    hidden_share = jnp.square(jax.nn.relu(share)).astype(jnp.bfloat16)
    projected = jnp.dot(
        lax.all_gather(hidden_share, "req", axis=1, tiled=True),
        down_weight,
        preferred_element_type=jnp.float32,
    )
    projected = head_total(projected)
    residual_out = (middle.astype(jnp.float32) + projected).astype(jnp.bfloat16)
    return (residual_out, state_out, window_mix[:, 1:], window_group[:, 1:])


def solution(mesh):
    return jax.shard_map(
        on_device,
        mesh=mesh,
        in_specs=(
            P(None, "req"),
            P("req"),
            P("req", "head", None, None),
            P("req", None, "head"),
            P("req", None, None, "head"),
            P("req"),
            P("req", None, "head"),
            P("req", None, "head"),
            P("req", "head"),
            P(None, "head"),
            P(None, None, "head"),
            P("head"),
            P(None, "head"),
            P("head"),
            P("head"),
            P("head"),
            P("head"),
            P("head", "req"),
            P("req"),
            P("req", "head"),
            P("head", "req"),
        ),
        out_specs=(
            P(None, "req"),
            P("req", "head", None, None),
            P("req", None, "head"),
            P("req", None, None, "head"),
        ),
        check_vma=False,
    )
```

profile of v0, /device:TPU:0, one launch (start us, length us, event | category | flops | bytes accessed | tf_op | source)
XLA Modules:
  0.0 373.0 jit_solution(13853456212551379219)
XLA Ops:
  7.3 1.3 copy.44
  8.5 1.1 fusion.24
  9.6 1.1 fusion.26
  10.8 4.6 %copy.43 = bf16[64,8,2,2048]{3,1,2,0:T(8,128)(2,1)S(1)} copy(bf16[64,8,2,2048]{3,2,1,0:T(2,128)(2,1)} %bitcast.43) | data formatting | bytes 8388608
  15.4 0.7 fusion.28
  16.2 1.6 pad_maximum_fusion
  19.5 23.2 %psum.28 = f32[128]{0:T(128)S(1)} all-reduce(f32[128]{0:T(128)S(1)} %fusion.14), channel_id=1, replica_groups=mesh['req'=8,'head'=4] {'req'}, use_global_device_ids=true, to_apply=%region_2.0 | all-reduce | flops 128 | bytes 1024 | tf_op jit(solution)/shard_map/psum | solution.py:15
  43.0 47.4 %reduce-scatter.5.cloned.1.call-done = f32[16,4640]{1,0:T(8,128)} async-done(((f32[128,4640]{1,0:T(8,128)}), f32[16,4640]{1,0:T(8,128)}) %reduce-scatter.5.cloned.1.call-update) | async-done | bytes 296976 | tf_op jit(solution)/shard_map/reduce_scatter | solution.py:70
  90.4 1.1 broadcast_multiply_fusion.1
  91.5 0.7 mul.216
  94.8 0.8 fusion.8
  95.7 0.9 broadcast_multiply_fusion.2
  96.6 42.1 %fusion = f32[16,2,1,16,64]{4,2,3,1,0:T(1,128)S(1)} fusion(f32[16,2,16,64,128]{4,3,2,1,0:T(8,128)} %bitcast.41, f32[16,2,128]{2,1,0:T(2,128)} %bitcast.52, f32[16,2,16,64]{3,2,1,0:T(8,128)S(1)} %broadcast_multiply_fusion.2, f32[16,2,16]{2,1,0:T(2,128)} %mul.216, f32[16,2,256]{2,1,0:T(2,128)} %copy-done.6), kind=kOutput, calls=%fused_computation.1 | convolution fusion | flops 62914560 | bytes 17088512 | tf_op jit(solution)/shard_map/rgepn,rgn->rgep/dot_general | solution.py:94
  138.8 0.8 multiply_add_fusion.1
  139.6 1.1 reshape.128
  140.7 0.8 mul.242
  141.5 1.0 reduce_sum.53
  142.7 0.8 multiply_convert_fusion
  143.4 31.4 %all_gather.6 = bf16[128,2048]{1,0:T(8,128)(2,1)S(1)} all-gather(bf16[16,2048]{1,0:T(8,128)(2,1)S(1)} %multiply_convert_fusion), channel_id=1, replica_groups=mesh['req'=8,'head'=4] {'req'}, dimensions={0}, use_global_device_ids=true | all-gather | bytes 589824 | tf_op jit(solution)/shard_map/all_gather | solution.py:104
  174.9 1.2 fusion.33
  176.3 30.6 %all-reduce.3.cloned.1.call-done = f32[128,512]{1,0:T(8,128)} async-done(((f32[128,512]{1,0:T(8,128)}), f32[128,512]{1,0:T(8,128)}) %all-reduce.3.cloned.1.call-update) | async-done | bytes 262160 | tf_op jit(solution)/shard_map/psum | solution.py:23
  206.9 1.1 fusion.17
  208.0 6.4 %convolution_bitcast_fusion = f32[5376,128]{1,0:T(8,128)} fusion(bf16[512,5376]{1,0:T(8,128)(2,1)} %param.40, bf16[128,512]{1,0:T(8,128)(2,1)S(1)} %get-tuple-element.5, f32[512]{0:T(512)} %param.39), kind=kOutput, calls=%fused_computation.8 | convolution fusion | flops 704839680 | bytes 8390656
  214.5 21.6 %psum.30 = f32[128]{0:T(128)S(1)} all-reduce(f32[128]{0:T(128)S(1)} %get-tuple-element.4), channel_id=1, replica_groups=mesh['req'=8,'head'=4] {'req'}, use_global_device_ids=true, to_apply=%region_9.10 | all-reduce | flops 128 | bytes 1024 | tf_op jit(solution)/shard_map/psum | solution.py:15
  236.1 49.4 %reduce-scatter.7.cloned.1.call-done = f32[672,128]{1,0:T(8,128)} async-done(((f32[5376,128]{1,0:T(8,128)}), f32[672,128]{1,0:T(8,128)}) %reduce-scatter.7.cloned.1.call-update) | async-done | bytes 344080
  285.5 1.7 fusion.12
  287.7 13.3 %multiply_add_fusion = f32[16,32,64,128]{3,2,1,0:T(8,128)} fusion(f32[16,32,64,128]{3,2,1,0:T(8,128)} %param.23, f32[16,32,128]{2,1,0:T(8,128)S(1)} %bitcast.46, f32[16,32,64]{2,1,0:T(8,128)S(1)} %multiply_multiply_fusion, f32[16,32]{1,0:T(8,128)S(1)} %get-tuple-element.6), kind=kLoop, calls=%fused_computation | loop fusion | flops 12582912 | bytes 33949696 | tf_op jit(solution)/shard_map/add | solution.py:93
  300.9 28.5 %all-gather.2.cloned.1.call-done = bf16[128,5376]{0,1:T(8,128)(2,1)} async-done(((bf16[128,672]{0,1:T(8,128)(2,1)}), bf16[128,5376]{0,1:T(8,128)(2,1)}) %all-gather.2.cloned.1.call-update) | async-done | bytes 1376272 | tf_op jit(solution)/shard_map/all_gather | solution.py:118
  329.5 4.6 %fusion.34 = f32[128,512]{1,0:T(8,128)} fusion(bf16[128,5376]{0,1:T(8,128)(2,1)} %all-gather.2.cloned.1.call-done, bf16[5376,512]{1,0:T(8,128)(2,1)} %param.41), kind=kOutput, calls=%fused_computation.66 | convolution fusion | flops 704643072 | bytes 7143424 | tf_op jit(solution)/shard_map/dot_general | solution.py:117
  334.1 0.8 fusion.9
  335.6 29.2 %all-reduce.5.cloned.1.call-done = f32[128,512]{1,0:T(8,128)} async-done(((f32[128,512]{1,0:T(8,128)}), f32[128,512]{1,0:T(8,128)}) %all-reduce.5.cloned.1.call-update) | async-done | bytes 262160 | tf_op jit(solution)/shard_map/psum | solution.py:23
  364.8 1.6 fusion.18
  (84 shorter events, 6.3 us)
Async XLA Ops:
  7.2 167.7 %copy-start = (bf16[2048,512]{1,0:T(8,128)(2,1)S(1)}, bf16[2048,512]{1,0:T(8,128)(2,1)}, u32[]{:S(2)}) copy-start(bf16[2048,512]{1,0:T(8,128)(2,1)} %param.38) | copy-start | bytes 6291460
  7.2 8.2 %copy-start.2 = (bf16[128,512]{1,0:T(8,128)(2,1)S(1)}, bf16[128,512]{1,0:T(8,128)(2,1)}, u32[]{:S(2)}) copy-start(bf16[128,512]{1,0:T(8,128)(2,1)} %param.21) | copy-start | bytes 393220
  7.2 8.2 %copy-start.14 = (f32[512]{0:T(512)S(1)}, f32[512]{0:T(512)}, u32[]{:S(2)}) copy-start(f32[512]{0:T(512)} %param.26) | copy-start | bytes 6148
  7.2 83.2 %reduce-scatter.5.cloned.1.call-start = ((), (), s32[]{:S(2)}) async-start(), calls=%async_computation.2 | async-start | bytes 2727936 | tf_op jit(solution)/shard_map/reduce_scatter | solution.py:70
  15.4 2.5 copy-start.19
  15.4 2.5 copy-start.20
  15.4 3.2 copy-start.21
  15.4 3.3 copy-start.12
  15.4 27.3 %copy-start.9 = (f32[16,3,2,256]{3,2,1,0:T(2,128)S(1)}, f32[16,3,2,256]{3,2,1,0:T(2,128)}, u32[]{:S(2)}) copy-start(f32[16,3,2,256]{3,2,1,0:T(2,128)} %param.25) | copy-start | bytes 294916
  15.4 27.4 %copy-start.3 = (f32[16,3,2048]{2,0,1:T(8,128)S(1)}, f32[16,3,2048]{2,0,1:T(8,128)}, u32[]{:S(2)}) copy-start(f32[16,3,2048]{2,0,1:T(8,128)} %param.24) | copy-start | bytes 1179652
  16.2 75.3 %copy-start.18 = (f32[32]{0:T(128)S(1)}, f32[32]{0:T(128)}, u32[]{:S(2)}) copy-start(f32[32]{0:T(128)} %param.34) | copy-start | bytes 388
  16.2 76.8 %copy-start.15 = (f32[4,2,256]{2,1,0:T(2,128)S(1)}, f32[4,2,256]{2,1,0:T(2,128)}, u32[]{:S(2)}) copy-start(f32[4,2,256]{2,1,0:T(2,128)} %param.31) | copy-start | bytes 24580
  16.2 76.9 %copy-start.16 = (f32[2,256]{1,0:T(2,128)S(1)}, f32[2,256]{1,0:T(2,128)}, u32[]{:S(2)}) copy-start(f32[2,256]{1,0:T(2,128)} %param.33) | copy-start | bytes 6148
  17.8 189.1 %all-reduce.3.cloned.1.call-start = ((), (), s32[]{:S(2)}) async-start(), calls=%async_computation.3 | async-start | bytes 524288 | tf_op jit(solution)/shard_map/psum | solution.py:23
  91.5 0.7 copy-start.10
  93.0 0.6 copy-start.4
  93.6 0.6 copy-start.6
  96.6 42.2 %copy-start.8 = (f32[2,16,64]{2,1,0:T(8,128)S(1)}, f32[2,16,64]{2,1,0:T(8,128)}, u32[]{:S(2)}) copy-start(f32[2,16,64]{2,1,0:T(8,128)} %add.116) | copy-start | bytes 24580
  96.6 42.1 %copy-start.17 = (f32[2,16]{1,0:T(2,128)S(1)}, f32[2,16]{1,0:T(2,128)}, u32[]{:S(2)}) copy-start(f32[2,16]{1,0:T(2,128)} %mul.236) | copy-start | bytes 388
  176.1 109.5 %reduce-scatter.7.cloned.1.call-start = ((), (), s32[]{:S(2)}) async-start(), calls=%async_computation.6 | async-start | bytes 3096576
  208.0 79.3 %copy-start.13 = (f32[2048]{0:T(1024)S(1)}, f32[2048]{0:T(1024)}, u32[]{:S(2)}) copy-start(f32[2048]{0:T(1024)} %param.32) | copy-start | bytes 24580
  208.0 79.5 %copy-start.11 = (f32[16,32]{1,0:T(8,128)S(1)}, f32[16,32]{1,0:T(8,128)}, u32[]{:S(2)}) copy-start(f32[16,32]{1,0:T(8,128)} %copy-done.10) | copy-start | bytes 6148
  208.0 79.6 %copy-start.7 = (f32[16,1,256]{2,1,0:T(1,128)S(1)}, f32[16,1,256]{2,1,0:T(1,128)}, u32[]{:S(2)}) copy-start(f32[16,1,256]{2,1,0:T(1,128)} %slice.35) | copy-start | bytes 49156
  214.4 115.1 %all-gather.2.cloned.1.call-start = ((), (), s32[]{:S(2)}) async-start(), calls=%async_computation.4 | async-start | bytes 1548288 | tf_op jit(solution)/shard_map/all_gather | solution.py:118
  287.2 77.6 %all-reduce.5.cloned.1.call-start = ((), (), s32[]{:S(2)}) async-start(), calls=%async_computation.5 | async-start | bytes 524288 | tf_op jit(solution)/shard_map/psum | solution.py:23
  287.7 78.8 %copy-start.1 = (bf16[2048,512]{1,0:T(8,128)(2,1)S(1)}, bf16[2048,512]{1,0:T(8,128)(2,1)}, u32[]{:S(2)}) copy-start(bf16[2048,512]{1,0:T(8,128)(2,1)} %param.38) | copy-start | bytes 6291460
  300.9 34.0 %copy-start.5 = (f32[16,1,2,256]{3,2,0,1:T(2,128)S(1)}, f32[16,1,2,256]{3,2,0,1:T(2,128)}, u32[]{:S(2)}) copy-start(f32[16,1,2,256]{3,2,0,1:T(2,128)} %copy-done.4) | copy-start | bytes 98308
Sparse Core Ops, SparseCore 0:
  18.0 72.3 reduce-scatter.4
  176.2 30.7 all-reduce.2
  214.5 70.9 reduce-scatter.6
  288.1 41.3 all-gather.1
  334.3 30.4 all-reduce.4
where the time goes:
time: 374 us; the launch traced here: 373 us
  waiting for transfers between devices  185 us (49%)
  blocking collectives  76.2 us (20%)
  matrix products  57.2 us (15%)
  other arithmetic  26.8 us (7%)
  between operations  14.2 us (4%)
  local copies, waits for them, and re-layouts  12.8 us (3%)
    psum x2, waiting for transfers between devices, head_total(): return lax.psum(partial_sum, 'head')  59.8 us
    unnamed x6, waiting for transfers between devices  49.5 us
    reduce_scatter x1, waiting for transfers between devices, on_device(): lax.psum_scatter(jnp.concatenate(pieces, axis=1), 'req', scatter_dimensio...  47.4 us
    psum x2, blocking collectives, norm_total(): return lax.psum(partial_sum, 'req')  44.8 us
    dot_general x1, matrix products, on_device(): jnp.einsum('rgepn,rgn->rgep', updated, c_vector, precision=lax.Precision....  42.1 us
    all_gather x1, blocking collectives, on_device(): lax.all_gather(normed_y, 'req', axis=0, tiled=True)  31.4 us
    all_gather x1, waiting for transfers between devices, on_device(): lax.all_gather(hidden_share, 'req', axis=1, tiled=True)  28.5 us
    add x1, other arithmetic, on_device(): updated = rate * prior + (stride * inputs)[..., None] * b_vector  13.3 us
  transfers between devices with their start and end apart: 5, of which 5 were waited for; matrix products, arithmetic and copies ran while one was open for 5% of the time, Pallas kernels for 0%

commit v1 on v0

v1 whole, which is shorter than its diff:
```python
import functools

import jax
import jax.numpy as jnp
from jax import lax
from jax.experimental import pallas as pl
from jax.experimental.pallas import tpu as pltpu
from jax.sharding import PartitionSpec as P

eps = 1e-05
MESH = pl.DeviceIdType.MESH
F32 = jnp.float32
BF16 = jnp.bfloat16
VMEM = pltpu.VMEM


def spans(total, size):
    return [(s, min(size, total - s)) for s in range(0, total, size)]


def remote(src, dst, send, recv, target):
    return pltpu.make_async_remote_copy(
        src_ref=src,
        dst_ref=dst,
        send_sem=send,
        recv_sem=recv,
        device_id=target,
        device_id_type=MESH,
    )


class Place:
    def __init__(self, n_req, n_head):
        self.n_hi = n_req // 2
        self.n_head = n_head
        req = lax.axis_index("req")
        self.head = lax.axis_index("head")
        self.req = req
        self.hi = req // 2
        self.lo = lax.rem(req, 2)
        self.pair = (self.hi * 2 + 1 - self.lo, self.head)

    def hi_at(self, step):
        return lax.rem(self.hi + step + self.n_hi, self.n_hi)

    def column(self, step):
        return (self.hi_at(step) * 2 + self.lo, self.head)

    def head_at(self, step):
        return lax.rem(self.head + step + self.n_head, self.n_head)

    def heads(self, step):
        return (self.req, self.head_at(step))

    def greet(self, with_heads):
        barrier = pltpu.get_barrier_semaphore()
        peers = [self.pair] + [self.column(k) for k in range(1, self.n_hi)]
        if with_heads:
            peers += [self.heads(k) for k in range(1, self.n_head)]
        for peer in peers:
            pl.semaphore_signal(barrier, inc=1, device_id=peer, device_id_type=MESH)
        pl.semaphore_wait(barrier, len(peers))


class Scatter:
    def __init__(self, place, index, cols, part, first, mid, second, sems):
        self.place = place
        self.part, self.first, self.mid, self.second = part, first, mid, second
        self.cols = cols
        pair_send, pair_recv, col_send, col_recv = sems
        n_hi = place.n_hi
        self.to_pair = remote(
            part.at[:, 1 - place.lo, :, cols],
            first.at[:, :, cols],
            pair_send.at[index],
            pair_recv.at[index],
            place.pair,
        )
        self.to_col = [
            remote(
                mid.at[place.hi_at(k), :, cols],
                second.at[k - 1, :, cols],
                col_send.at[index, k - 1],
                col_recv.at[index, k - 1],
                place.column(k),
            )
            for k in range(1, n_hi)
        ]

    def send_pair(self):
        self.to_pair.start()

    def send_column(self):
        place, cols = self.place, self.cols
        self.to_pair.wait_recv()
        for k, copy in enumerate(self.to_col):
            there = place.hi_at(k + 1)
            both = self.part[there, place.lo, :, cols].astype(F32) + self.first[there, :, cols].astype(F32)
            self.mid[there, :, cols] = both.astype(self.mid.dtype)
            copy.start()

    def total(self):
        place, cols = self.place, self.cols
        here = place.hi
        value = self.part[here, place.lo, :, cols].astype(F32) + self.first[here, :, cols].astype(F32)
        for k, copy in enumerate(self.to_col):
            copy.wait_recv()
            value = value + self.second[k, :, cols].astype(F32)
        return value

    def finish(self):
        self.to_pair.wait_send()
        for copy in self.to_col:
            copy.wait_send()


class Gather:
    def __init__(self, place, index, cols, every, sems):
        self.place = place
        col_send, col_recv, pair_send, pair_recv = sems
        n_hi = place.n_hi
        mine = every.at[place.hi, place.lo, :, cols]
        self.to_col = [
            remote(mine, mine, col_send.at[index, k - 1], col_recv.at[index, k - 1], place.column(k))
            for k in range(1, n_hi)
        ]
        self.to_pair = []
        self.from_pair = []
        for k in range(n_hi):
            block = every.at[place.hi_at(-k), place.lo, :, cols]
            self.to_pair.append(remote(block, block, pair_send.at[index, k], pair_recv.at[index, k], place.pair))
            landed = every.at[place.hi_at(-k), 1 - place.lo, :, cols]
            self.from_pair.append(remote(landed, landed, pair_send.at[index, k], pair_recv.at[index, k], place.pair))
        self.from_col = []
        for k in range(1, n_hi):
            block = every.at[place.hi_at(-k), place.lo, :, cols]
            self.from_col.append(
                remote(block, block, col_send.at[index, k - 1], col_recv.at[index, k - 1], place.column(k))
            )

    def send(self):
        for copy in self.to_col:
            copy.start()
        self.to_pair[0].start()

    def forward(self):
        for k, copy in enumerate(self.from_col):
            copy.wait_recv()
            self.to_pair[k + 1].start()

    def land(self):
        for copy in self.from_pair:
            copy.wait_recv()

    def finish(self):
        for copy in self.to_col + self.to_pair:
            copy.wait_send()


def project_kernel(
    n_req, n_head, width_all, chunks, part, squares, out, first, mid, second, first_sq, mid_sq, second_sq,
    pair_send, pair_recv, col_send, col_recv,
):
    place = Place(n_req, n_head)
    place.greet(False)
    sems = (pair_send, pair_recv, col_send, col_recv)
    norm = Scatter(place, len(chunks), slice(None), squares, first_sq, mid_sq, second_sq, sems)
    moves = [
        Scatter(place, c, pl.ds(s, w), part, first, mid, second, sems) for c, (s, w) in enumerate(chunks)
    ]
    norm.send_pair()
    for move in moves:
        move.send_pair()
    norm.send_column()
    inverse = None
    for c in range(len(moves) + 1):
        if c < len(moves):
            moves[c].send_column()
        if c == 0:
            inverse = lax.rsqrt(norm.total()[:, :1] / width_all + eps)
        else:
            s, w = chunks[c - 1]
            out[:, s : s + w] = moves[c - 1].total() * inverse
    norm.finish()
    for move in moves:
        move.finish()


def project(part, squares, n_req, n_head, width_all):
    rows, n = part.shape
    rows_dev = rows // n_req
    n_hi = n_req // 2
    chunks = spans(n, 1024)
    count = len(chunks) + 1
    dma = pltpu.SemaphoreType.DMA
    vmem = pl.BlockSpec(memory_space=VMEM)
    return pl.pallas_call(
        functools.partial(project_kernel, n_req, n_head, width_all, chunks),
        out_shape=jax.ShapeDtypeStruct((rows_dev, n), F32),
        in_specs=[vmem, vmem],
        out_specs=vmem,
        scratch_shapes=[
            VMEM((n_hi, rows_dev, n), BF16),
            VMEM((n_hi, rows_dev, n), BF16),
            VMEM((n_hi - 1, rows_dev, n), BF16),
            VMEM((n_hi, rows_dev, 128), F32),
            VMEM((n_hi, rows_dev, 128), F32),
            VMEM((n_hi - 1, rows_dev, 128), F32),
            dma((count,)),
            dma((count,)),
            dma((count, n_hi - 1)),
            dma((count, n_hi - 1)),
        ],
        compiler_params=pltpu.CompilerParams(
            collective_id=0, has_side_effects=True, vmem_limit_bytes=48 * 1024 * 1024
        ),
    )(part.reshape(n_hi, 2, rows_dev, n), squares.reshape(n_hi, 2, rows_dev, 128))


def state_kernel(groups, per_group, head_dim, decay, stride_t, b_all, c_all, prior, updated, readout, left):
    row = pl.program_id(0)
    rows, state = b_all.shape[0], prior.shape[3]

    @pl.when(row == 0)
    def _():
        wide = stride_t[...]
        high = wide.astype(BF16)
        low = (wide - high.astype(F32)).astype(BF16)
        lane = lax.broadcasted_iota(jnp.int32, wide.shape, 1)
        left[...] = jnp.where(lane < 2 * rows, high.astype(F32), low.astype(F32)).astype(BF16)

    line = lax.broadcasted_iota(jnp.int32, (3 * rows, state), 0)
    chosen = lax.rem(line, rows) == row
    middle = (line >= rows) & (line < 2 * rows)
    own_row = lax.broadcasted_iota(jnp.int32, (rows, state), 0) == row
    span = per_group * head_dim
    for g in range(groups):
        b = b_all[:, g * state : (g + 1) * state]
        b = jnp.concatenate([b, b, b], axis=0)
        b_high = b.astype(BF16).astype(F32)
        b = jnp.where(chosen, jnp.where(middle, b - b_high, b_high), 0.0).astype(BF16)
        c = c_all[:, g * state : (g + 1) * state]
        c = jnp.sum(jnp.where(own_row, c, 0.0), axis=0, keepdims=True)
        c_high = c.astype(BF16).astype(F32)
        place = lax.broadcasted_iota(jnp.int32, (16, state), 0)
        c = jnp.where(place == 0, c_high, jnp.where(place == 1, c - c_high, 0.0)).astype(BF16)
        outer = jnp.dot(left[g * span : (g + 1) * span, :], b, preferred_element_type=F32)
        pieces = []
        for e in range(per_group):
            h = g * per_group + e
            value = decay[row, h] * prior[0, h] + outer[e * head_dim : (e + 1) * head_dim]
            updated[0, h] = value
            pieces.append(value.astype(BF16))
        block = jnp.concatenate(pieces, axis=0)
        found = lax.dot_general(c, block, (((1,), (1,)), ((), ())), preferred_element_type=F32)
        readout[0, :, g * span : (g + 1) * span] = jnp.sum(found, axis=0, keepdims=True)


def state_step(decay, stride, b_vector, c_vector, prior):
    rows, heads, head_dim, state = prior.shape
    groups = b_vector.shape[1] // state
    turned = stride.T
    vmem = pl.BlockSpec(memory_space=VMEM)
    block = pl.BlockSpec((1, heads, head_dim, state), lambda r: (r, 0, 0, 0))
    mix = heads * head_dim
    updated, readout = pl.pallas_call(
        functools.partial(state_kernel, groups, heads // groups, head_dim),
        grid=(rows,),
        out_shape=(
            jax.ShapeDtypeStruct(prior.shape, F32),
            jax.ShapeDtypeStruct((rows, 1, mix), F32),
        ),
        in_specs=[pl.BlockSpec(memory_space=pltpu.SMEM), vmem, vmem, vmem, block],
        out_specs=(block, pl.BlockSpec((1, 1, mix), lambda r: (r, 0, 0))),
        scratch_shapes=[VMEM((mix, 3 * rows), BF16)],
        compiler_params=pltpu.CompilerParams(vmem_limit_bytes=48 * 1024 * 1024),
        cost_estimate=pl.CostEstimate(flops=4 * prior.size * 48, bytes_accessed=8 * prior.size, transcendentals=0),
    )(decay, jnp.concatenate([turned, turned, turned], axis=1), b_vector, c_vector, prior)
    return updated, readout.reshape(rows, mix)


def mlp_kernel(
    n_req, n_head, width_all, y_chunks, chunks,
    residual, y_own, gain, out_w, up_w, down_w, out,
    out_v, up_v, down_v, y_all, partial, partial_in, mid_all, act, first, mid, second,
    squares, first_sq, mid_sq, second_sq, hidden, result,
    load, y_cs, y_cr, y_ps, y_pr, h_send, h_recv, g_send, g_recv,
    s_ps, s_pr, s_cs, s_cr, a_cs, a_cr, a_ps, a_pr, h2_send, h2_recv, g2_send, g2_recv,
):
    loads = [
        pltpu.make_async_copy(src, dst, load.at[i])
        for i, (src, dst) in enumerate([(out_w, out_v), (up_w, up_v), (down_w, down_v)])
    ]
    for copy in loads:
        copy.start()
    place = Place(n_req, n_head)
    place.greet(True)
    n_hi = place.n_hi
    rows = residual.shape[0]
    width = residual.shape[1]
    rows_dev = rows // n_req
    rows_head = rows // n_head
    at_head = pl.multiple_of(place.head * rows_head, rows_head)

    def spread(send_from, land_in, send, recv):
        copies = []
        for k in range(1, n_head):
            copies.append(
                remote(
                    send_from(place.head_at(k)), land_in(k), send.at[k - 1], recv.at[k - 1], place.heads(k)
                )
            )
            copies[-1].start()
        return copies

    def block_of(ref, index):
        return ref.at[pl.ds(pl.multiple_of(index * rows_head, rows_head), rows_head)]

    def head_sum(send, recv, landing):
        copies = spread(lambda h: block_of(partial, h), lambda k: landing.at[k - 1], send, recv)
        total = partial[pl.ds(at_head, rows_head), :].astype(F32)
        for k, copy in enumerate(copies):
            copy.wait_recv()
            total = total + landing[k].astype(F32)
        return total, copies

    def head_gather(ref, send, recv):
        mine = block_of(ref, place.head)
        copies = spread(lambda h: mine, lambda k: mine, send, recv)
        for k in range(1, n_head):
            there = block_of(ref, place.head_at(-k))
            remote(there, there, send.at[k - 1], recv.at[k - 1], place.heads(k)).wait_recv()
        return copies

    pending = []
    y_all[place.hi, place.lo] = y_own[...]
    gathers = [
        Gather(place, c, pl.ds(s, w), y_all, (y_cs, y_cr, y_ps, y_pr)) for c, (s, w) in enumerate(y_chunks)
    ]
    for move in gathers:
        move.send()
    for move in gathers:
        move.forward()
    loads[0].wait()
    mixer = None
    for move, (s, w) in zip(gathers, y_chunks):
        move.land()
        term = jnp.dot(
            y_all[:, :, :, s : s + w].reshape(rows, w), out_v[s : s + w, :], preferred_element_type=F32
        )
        mixer = term if mixer is None else mixer + term
    partial[...] = mixer.astype(BF16)
    total, copies = head_sum(h_send, h_recv, partial_in.at[0])
    pending += gathers
    for copy in copies:
        copy.wait_send()
    mid_all[pl.ds(at_head, rows_head), :] = (
        residual[pl.ds(at_head, rows_head), :].astype(F32) + total
    ).astype(BF16)
    copies = head_gather(mid_all, g_send, g_recv)
    for copy in copies:
        copy.wait_send()

    wide = mid_all[...].astype(F32)
    sums = jnp.sum(wide * wide, axis=1, keepdims=True)
    squares[...] = jnp.broadcast_to(sums, (rows, 128)).reshape(n_hi, 2, rows_dev, 128)
    sems = (s_ps, s_pr, s_cs, s_cr)
    norm = Scatter(place, len(chunks), slice(None), squares, first_sq, mid_sq, second_sq, sems)
    norm.send_pair()
    scaled = (wide * gain[...]).astype(BF16)
    moves = []
    shares = []
    loads[1].wait()
    for c, (s, w) in enumerate(chunks):
        piece = jnp.dot(scaled, up_v[:, s : s + w], preferred_element_type=F32).astype(BF16)
        act[:, :, :, s : s + w] = piece.reshape(n_hi, 2, rows_dev, w)
        moves.append(Scatter(place, c, pl.ds(s, w), act, first, mid, second, sems))
        moves[-1].send_pair()
        shares.append(Gather(place, c, pl.ds(s, w), hidden, (a_cs, a_cr, a_ps, a_pr)))
    norm.send_column()
    loads[2].wait()
    count = len(chunks)
    inverse = None
    projected = None
    for step in range(count + 3):
        if step < count:
            moves[step].send_column()
        c = step - 1
        if 0 <= c < count:
            if inverse is None:
                inverse = lax.rsqrt(norm.total()[:, :1] / width_all + eps)
            s, w = chunks[c]
            share = jnp.maximum(moves[c].total() * inverse, 0.0)
            hidden[place.hi, place.lo, :, pl.ds(s, w)] = (share * share).astype(BF16)
            shares[c].send()
        c = step - 2
        if 0 <= c < count:
            shares[c].forward()
        c = step - 3
        if 0 <= c < count:
            shares[c].land()
            s, w = chunks[c]
            term = jnp.dot(
                hidden[:, :, :, s : s + w].reshape(rows, w), down_v[s : s + w, :], preferred_element_type=F32
            )
            projected = term if projected is None else projected + term
    partial[...] = projected.astype(BF16)
    total, copies = head_sum(h2_send, h2_recv, partial_in.at[1])
    for copy in copies:
        copy.wait_send()
    result[pl.ds(at_head, rows_head), :] = (
        mid_all[pl.ds(at_head, rows_head), :].astype(F32) + total
    ).astype(BF16)
    copies = head_gather(result, g2_send, g2_recv)
    out[...] = result[...]
    for copy in copies:
        copy.wait_send()
    norm.finish()
    for move in pending + moves + shares:
        move.finish()


def mlp(residual, y_own, gain, out_w, up_w, down_w, n_req, n_head, width_all):
    rows, width = residual.shape
    rows_dev, mix = y_own.shape
    ff = up_w.shape[1]
    n_hi = n_req // 2
    y_chunks = spans(mix, 1024)
    chunks = spans(ff, 896)
    count, y_count = len(chunks), len(y_chunks)
    rows_head = rows // n_head
    dma = pltpu.SemaphoreType.DMA
    vmem = pl.BlockSpec(memory_space=VMEM)
    anywhere = pl.BlockSpec(memory_space=pl.ANY)
    n_col, n_side = n_hi - 1, n_head - 1
    return pl.pallas_call(
        functools.partial(mlp_kernel, n_req, n_head, width_all, y_chunks, chunks),
        out_shape=jax.ShapeDtypeStruct((rows, width), BF16),
        in_specs=[vmem, vmem, vmem, anywhere, anywhere, anywhere],
        out_specs=vmem,
        scratch_shapes=[
            VMEM(out_w.shape, BF16),
            VMEM(up_w.shape, BF16),
            VMEM(down_w.shape, BF16),
            VMEM((n_hi, 2, rows_dev, mix), BF16),
            VMEM((rows, width), BF16),
            VMEM((2, n_side, rows_head, width), BF16),
            VMEM((rows, width), BF16),
            VMEM((n_hi, 2, rows_dev, ff), BF16),
            VMEM((n_hi, rows_dev, ff), BF16),
            VMEM((n_hi, rows_dev, ff), BF16),
            VMEM((n_col, rows_dev, ff), BF16),
            VMEM((n_hi, 2, rows_dev, 128), F32),
            VMEM((n_hi, rows_dev, 128), F32),
            VMEM((n_hi, rows_dev, 128), F32),
            VMEM((n_col, rows_dev, 128), F32),
            VMEM((n_hi, 2, rows_dev, ff), BF16),
            VMEM((rows, width), BF16),
            dma((3,)),
            dma((y_count, n_col)),
            dma((y_count, n_col)),
            dma((y_count, n_hi)),
            dma((y_count, n_hi)),
            dma((n_side,)),
            dma((n_side,)),
            dma((n_side,)),
            dma((n_side,)),
            dma((count + 1,)),
            dma((count + 1,)),
            dma((count + 1, n_col)),
            dma((count + 1, n_col)),
            dma((count, n_col)),
            dma((count, n_col)),
            dma((count, n_hi)),
            dma((count, n_hi)),
            dma((n_side,)),
            dma((n_side,)),
            dma((n_side,)),
            dma((n_side,)),
        ],
        compiler_params=pltpu.CompilerParams(
            collective_id=1, has_side_effects=True, vmem_limit_bytes=52 * 1024 * 1024
        ),
    )(residual, y_own, gain.reshape(1, width), out_w, up_w, down_w)


def on_device(
    residual,
    lengths,
    ssm_state,
    tail_mix,
    tail_group,
    norm_first,
    mix_weight,
    group_weight,
    step_weight,
    conv_mix,
    conv_group,
    bias_mix,
    bias_group,
    step_bias,
    decay_log,
    skip_gain,
    gate_gain,
    out_weight,
    norm_second,
    up_weight,
    down_weight,
):
    rows_dev, heads_dev, head_dim, state_size = ssm_state.shape
    mix_dev = mix_weight.shape[2]
    group_dev = group_weight.shape[2]
    groups_dev = group_dev // state_size
    rows, width_dev = residual.shape
    n_req, n_head = lax.axis_size("req"), lax.axis_size("head")
    width_all = width_dev * n_req
    taps_all = conv_mix.shape[0]
    wide = residual.astype(F32)
    squares = jnp.broadcast_to(jnp.sum(wide * wide, axis=1, keepdims=True), (rows, 128))
    scaled = (wide * norm_first).astype(BF16)
    steps_pad = -heads_dev % 128
    pieces = [
        jnp.dot(scaled, mix_weight[:, 0], preferred_element_type=F32),
        jnp.dot(scaled, mix_weight[:, 1], preferred_element_type=F32),
        jnp.dot(scaled, group_weight[:, 0], preferred_element_type=F32),
        jnp.dot(scaled, group_weight[:, 1], preferred_element_type=F32),
        jnp.pad(jnp.dot(scaled, step_weight, preferred_element_type=F32), ((0, 0), (0, steps_pad))),
    ]
    part = jnp.concatenate([piece.astype(BF16) for piece in pieces], axis=1)
    sums = project(part, squares, n_req, n_head, width_all)
    gate_z = sums[:, :mix_dev]
    mix_in = sums[:, mix_dev : 2 * mix_dev]
    group_in = sums[:, 2 * mix_dev : 2 * mix_dev + 2 * group_dev].reshape(rows_dev, 2, group_dev)
    step_raw = sums[:, 2 * mix_dev + 2 * group_dev : 2 * mix_dev + 2 * group_dev + heads_dev]
    valid = jnp.minimum(lengths, taps_all - 1)
    slots = jnp.arange(taps_all - 1)
    keep = (slots[None, :] >= (taps_all - 1 - valid)[:, None]).astype(F32)
    window_mix = jnp.concatenate([tail_mix * keep[:, :, None], mix_in[:, None, :]], axis=1)
    window_group = jnp.concatenate([tail_group * keep[:, :, None, None], group_in[:, None]], axis=1)
    conv_x = jax.nn.silu(jnp.sum(window_mix * conv_mix[None], axis=1) + bias_mix)
    conv_bc = jax.nn.silu(jnp.sum(window_group * conv_group[None], axis=1) + bias_group)
    step_size = jax.nn.softplus(step_raw + step_bias)
    alive = (lengths > 0).astype(F32)
    decay = jnp.exp(-step_size * jnp.exp(decay_log)) * alive[:, None]
    stride = jnp.repeat(step_size, head_dim, axis=1) * conv_x
    state_out, readout = state_step(decay, stride, conv_bc[:, 0], conv_bc[:, 1], ssm_state)
    mixed = readout + jnp.repeat(skip_gain, head_dim)[None, :] * conv_x
    gated = mixed * jax.nn.silu(gate_z)
    grouped = gated.reshape(rows_dev, groups_dev, -1)
    inverse = lax.rsqrt(jnp.mean(grouped * grouped, axis=2, keepdims=True) + eps)
    normed_y = ((grouped * inverse).reshape(rows_dev, mix_dev) * gate_gain).astype(BF16)
    residual_out = mlp(
        residual, normed_y, norm_second, out_weight, up_weight, down_weight, n_req, n_head, width_all
    )
    return (residual_out, state_out, window_mix[:, 1:], window_group[:, 1:])


def solution(mesh):
    return jax.shard_map(
        on_device,
        mesh=mesh,
        in_specs=(
            P(None, "req"),
            P("req"),
            P("req", "head", None, None),
            P("req", None, "head"),
            P("req", None, None, "head"),
            P("req"),
            P("req", None, "head"),
            P("req", None, "head"),
            P("req", "head"),
            P(None, "head"),
            P(None, None, "head"),
            P("head"),
            P(None, "head"),
            P("head"),
            P("head"),
            P("head"),
            P("head"),
            P("head", "req"),
            P("req"),
            P("req", "head"),
            P("head", "req"),
        ),
        out_specs=(
            P(None, "req"),
            P("req", "head", None, None),
            P("req", None, "head"),
            P("req", None, None, "head"),
        ),
        check_vma=False,
    )
```

time: 374 us -> 140 us (0.37)
  waiting for transfers between devices: 185 us -> 0 us
  Pallas kernels: 0 us -> 115 us
  blocking collectives: 76.2 us -> 0 us
  matrix products: 57.2 us -> 4.19 us
  other arithmetic: 26.8 us -> 6.45 us
  between operations: 14.2 us -> 0.99 us
    pallas_call x0 -> x3, Pallas kernels: none -> 115 us  [the longest x1 68.2 us: mlp(): pl.pallas_call(functools.partial(mlp_kernel, n_req, n_head, width_all, y_...]
    psum x2 -> x0, waiting for transfers between devices: 59.8 us -> none  [head_total(): return lax.psum(partial_sum, 'head')]
    unnamed x6 -> x0, waiting for transfers between devices: 49.5 us -> none
    reduce_scatter x1 -> x0, waiting for transfers between devices: 47.4 us -> none  [on_device(): lax.psum_scatter(jnp.concatenate(pieces, axis=1), 'req', scatter_dimensio...]
    dot_general x6 -> x5, matrix products: 50.8 us -> 4.19 us  [the longest x1 1.37 us: on_device(): jnp.dot(scaled, mix_weight[:, 1], preferred_element_type=F32)]
    psum x2 -> x0, blocking collectives: 44.8 us -> none  [norm_total(): return lax.psum(partial_sum, 'req')]
    all_gather x1 -> x0, blocking collectives: 31.4 us -> none  [on_device(): lax.all_gather(normed_y, 'req', axis=0, tiled=True)]
    all_gather x1 -> x0, waiting for transfers between devices: 28.5 us -> none  [on_device(): lax.all_gather(hidden_share, 'req', axis=1, tiled=True)]
  transfers between devices with their start and end apart: 5 -> 0, of which waited for: 5 -> 0; matrix products, arithmetic and copies ran while one was open for 5% -> 0% of each run, Pallas kernels for 0% -> 0%
where the time goes in v1:
time: 140 us; the launch traced here: 139 us
  Pallas kernels  115 us (82%)
  local copies, waits for them, and re-layouts  13.1 us (9%)
  other arithmetic  6.45 us (5%)
  matrix products  4.19 us (3%)
    pallas_call x1, Pallas kernels, mlp(): pl.pallas_call(functools.partial(mlp_kernel, n_req, n_head, width_all, y_...  68.2 us
    pallas_call x1, Pallas kernels, project(): pl.pallas_call(functools.partial(project_kernel, n_req, n_head, width_all...  27 us
    pallas_call x1, Pallas kernels, state_step(): pl.pallas_call(functools.partial(state_kernel, groups, heads // groups, h...  19.5 us
    slice x1, local copies, waits for them, and re-layouts, on_device(): mix_weight[:, 1]  8.85 us

profile of v1, /device:TPU:0, one launch (start us, length us, event | category | flops | bytes accessed | tf_op | source)
XLA Modules:
  0.0 139.4 jit_solution(2803224978335850589)
XLA Ops:
  0.7 0.7 exp.22
  1.4 0.7 minimum_subtract_fusion
  2.0 0.7 compare_convert_fusion
  2.7 1.0 fusion.8
  3.7 0.1 broadcast_in_dim.10
  3.8 0.1 copy.51
  3.9 1.1 convolution_convert_fusion.4
  5.0 0.7 broadcast_in_dim.14
  5.8 0.1 copy.60
  5.9 0.1 broadcast_in_dim.11.squares
  6.0 1.0 broadcast_multiply_fusion.1
  7.0 1.1 broadcast_multiply_fusion
  8.1 0.7 fusion.22
  8.9 8.9 %fusion.21 = (bf16[512,1,2048]{2,1,0:T(2,128)(2,1)S(1)}, bf16[512,1,2048]{2,1,0:T(2,128)(2,1)S(1)}) fusion(bf16[512,2,2048]{2,1,0:T(2,128)(2,1)} %param.27), kind=kLoop, calls=%fused_computation.51 | loop fusion | bytes 8388608 | tf_op jit(solution)/shard_map/slice | solution.py:524
  17.7 1.4 fusion.1
  19.1 1.4 fusion
  20.5 0.2 fusion.2
  20.7 0.2 fusion.3
  21.0 27.0 %shard_map.228 = f32[16,4736]{1,0:T(8,128)S(1)} custom-call(bf16[4,2,16,4736]{3,2,1,0:T(8,128)(2,1)S(1)} %bitcast.31, f32[4,2,16,128]{3,2,1,0:T(8,128)S(1)} %broadcast_in_dim.11.squares), custom_call_target="tpu_custom_call" | custom-call | tf_op jit(solution)/shard_map/pallas_call | solution.py:197
  48.2 0.1 fusion.11
  48.2 0.7 fusion.12
  49.1 0.8 fusion.6
  49.8 0.1 broadcast_in_dim.12
  50.0 0.1 reshape.92
  50.2 0.3 copy.54.stride_t
  50.5 19.5 %shard_map.229 = (f32[16,32,64,128]{3,2,1,0:T(8,128)}, f32[16,1,2048]{2,1,0:T(1,128)S(1)}) custom-call(f32[16,32]{1,0:T(8,128)S(1)} %get-tuple-element.10.decay, f32[2048,48]{1,0:T(8,128)S(1)} %copy.54.stride_t, f32[16,256]{1,0:T(8,128)S(1)} %get-tuple-element.17.b_all, f32[16,256]{1,0:T(8,128)S(1)} %get-tuple-element.16.c_all, f32[16,32,64,128]{3,2,1,0:T(8,128)} %prior.1), custom_call_target="tpu_custom_call" | custom-call | flops 805306368 | bytes 33554432 | tf_op jit(solution)/shard_map/pallas_call | solution.py:266
  70.0 0.1 fusion.19
  70.1 0.1 mul.135
  70.2 0.1 reduce_sum.39
  70.4 0.1 mul.136
  70.6 68.2 %shard_map.230 = bf16[128,512]{1,0:T(8,128)(2,1)S(1)} custom-call(bf16[128,512]{1,0:T(8,128)(2,1)S(1)} %copy-done.2, bf16[16,2048]{1,0:T(8,128)(2,1)S(1)} %multiply_convert_fusion.y_own, f32[1,512]{1,0:T(1,128)S(1)} %bitcast.32, bf16[2048,512]{1,0:T(8,128)(2,1)} %out_w.1, bf16[512,5376]{1,0:T(8,128)(2,1)} %up_w.1, bf16[5376,512]{1,0:T(8,128)(2,1)} %down_w.1), custom_call_target="tpu_custom_call" | custom-call | tf_op jit(solution)/shard_map/pallas_call | solution.py:436
  138.8 0.7 copy.80
  (39 shorter events, 0.5 us)
Async XLA Ops:
  0.6 3.3 %copy-start = (bf16[512,32]{0,1:T(8,128)(2,1)S(1)}, bf16[512,32]{0,1:T(8,128)(2,1)}, u32[]{:S(2)}) copy-start(bf16[512,32]{0,1:T(8,128)(2,1)} %param.29) | copy-start | bytes 98308
  0.6 7.4 %copy-start.4 = (bf16[512,2,256]{2,1,0:T(2,128)(2,1)S(1)}, bf16[512,2,256]{2,1,0:T(2,128)(2,1)}, u32[]{:S(2)}) copy-start(bf16[512,2,256]{2,1,0:T(2,128)(2,1)} %param.28) | copy-start | bytes 1572868
  8.8 8.9 %copy-start.2 = (bf16[128,512]{1,0:T(8,128)(2,1)S(1)}, bf16[128,512]{1,0:T(8,128)(2,1)}, u32[]{:S(2)}) copy-start(bf16[128,512]{1,0:T(8,128)(2,1)} %residual.1) | copy-start | bytes 393220
  8.8 8.9 %copy-start.11 = (f32[512]{0:T(512)S(1)}, f32[512]{0:T(512)}, u32[]{:S(2)}) copy-start(f32[512]{0:T(512)} %param.26) | copy-start | bytes 6148
  20.5 27.5 %copy-start.10 = (f32[32]{0:T(128)S(1)}, f32[32]{0:T(128)}, u32[]{:S(2)}) copy-start(f32[32]{0:T(128)} %param.34) | copy-start | bytes 388
  20.5 27.6 %copy-start.7 = (f32[4,2,256]{2,1,0:T(2,128)S(1)}, f32[4,2,256]{2,1,0:T(2,128)}, u32[]{:S(2)}) copy-start(f32[4,2,256]{2,1,0:T(2,128)} %param.31) | copy-start | bytes 24580
  20.5 28.4 %copy-start.9 = (f32[2,256]{1,0:T(2,128)S(1)}, f32[2,256]{1,0:T(2,128)}, u32[]{:S(2)}) copy-start(f32[2,256]{1,0:T(2,128)} %param.33) | copy-start | bytes 6148
  20.5 28.5 %copy-start.6 = (f32[4,2048]{1,0:T(4,128)S(1)}, f32[4,2048]{1,0:T(4,128)}, u32[]{:S(2)}) copy-start(f32[4,2048]{1,0:T(4,128)} %param.30) | copy-start | bytes 98308
  21.0 29.1 %copy-start.5 = (f32[2048]{0:T(1024)S(1)}, f32[2048]{0:T(1024)}, u32[]{:S(2)}) copy-start(f32[2048]{0:T(1024)} %param.32) | copy-start | bytes 24580
  50.5 20.0 %copy-start.8 = (f32[2048]{0:T(1024)S(1)}, f32[2048]{0:T(1024)}, u32[]{:S(2)}) copy-start(f32[2048]{0:T(1024)} %param.37) | copy-start | bytes 24580
  50.5 20.0 %copy-start.3 = (f32[512]{0:T(512)S(1)}, f32[512]{0:T(512)}, u32[]{:S(2)}) copy-start(f32[512]{0:T(512)} %param.39) | copy-start | bytes 6148
  70.6 68.9 %copy-start.1 = (bf16[512,32]{0,1:T(8,128)(2,1)S(1)}, bf16[512,32]{0,1:T(8,128)(2,1)}, u32[]{:S(2)}) copy-start(bf16[512,32]{0,1:T(8,128)(2,1)} %param.29) | copy-start | bytes 98308

commit v2 on v1

--- a/solution.py
+++ b/solution.py
@@ -158,19 +158,38 @@
 
 
 def project_kernel(
-    n_req, n_head, width_all, chunks, part, squares, out, first, mid, second, first_sq, mid_sq, second_sq,
+    n_req, n_head, width_all, chunks, residual, gain, mix_w, group_w, step_w, out,
+    part, first, mid, second, squares, first_sq, mid_sq, second_sq,
     pair_send, pair_recv, col_send, col_recv,
 ):
     place = Place(n_req, n_head)
     place.greet(False)
     sems = (pair_send, pair_recv, col_send, col_recv)
+    n_hi = place.n_hi
+    rows = residual.shape[0]
+    rows_dev = rows // n_req
+    wide = residual[...].astype(F32)
+    sums = jnp.sum(wide * wide, axis=1, keepdims=True)
+    squares[...] = jnp.broadcast_to(sums, (rows, 128)).reshape(n_hi, 2, rows_dev, 128)
     norm = Scatter(place, len(chunks), slice(None), squares, first_sq, mid_sq, second_sq, sems)
-    moves = [
-        Scatter(place, c, pl.ds(s, w), part, first, mid, second, sems) for c, (s, w) in enumerate(chunks)
-    ]
     norm.send_pair()
-    for move in moves:
-        move.send_pair()
+    scaled = (wide * gain[...]).astype(BF16)
+    mix = mix_w.shape[1]
+    moves = []
+    for c, (s, w) in enumerate(chunks):
+        if s < mix:
+            product = jnp.dot(scaled, mix_w[:, s : s + w], preferred_element_type=F32)
+        else:
+            product = jnp.concatenate(
+                [
+                    jnp.dot(scaled, group_w[...], preferred_element_type=F32),
+                    jnp.dot(scaled, step_w[...], preferred_element_type=F32),
+                ],
+                axis=1,
+            )
+        part[:, :, :, s : s + w] = product.astype(BF16).reshape(n_hi, 2, rows_dev, w)
+        moves.append(Scatter(place, c, pl.ds(s, w), part, first, mid, second, sems))
+        moves[-1].send_pair()
     norm.send_column()
     inverse = None
     for c in range(len(moves) + 1):
@@ -186,23 +205,27 @@
         move.finish()
 
 
-def project(part, squares, n_req, n_head, width_all):
-    rows, n = part.shape
+def project(residual, gain, mix_w, group_w, step_w, n_req, n_head, width_all):
+    rows, width = residual.shape
+    mix, rest = mix_w.shape[1], group_w.shape[1] + step_w.shape[1]
+    n = mix + rest
     rows_dev = rows // n_req
     n_hi = n_req // 2
-    chunks = spans(n, 1024)
+    chunks = spans(mix, 1024) + [(mix, rest)]
     count = len(chunks) + 1
     dma = pltpu.SemaphoreType.DMA
     vmem = pl.BlockSpec(memory_space=VMEM)
     return pl.pallas_call(
         functools.partial(project_kernel, n_req, n_head, width_all, chunks),
         out_shape=jax.ShapeDtypeStruct((rows_dev, n), F32),
-        in_specs=[vmem, vmem],
+        in_specs=[vmem] * 5,
         out_specs=vmem,
         scratch_shapes=[
+            VMEM((n_hi, 2, rows_dev, n), BF16),
             VMEM((n_hi, rows_dev, n), BF16),
             VMEM((n_hi, rows_dev, n), BF16),
             VMEM((n_hi - 1, rows_dev, n), BF16),
+            VMEM((n_hi, 2, rows_dev, 128), F32),
             VMEM((n_hi, rows_dev, 128), F32),
             VMEM((n_hi, rows_dev, 128), F32),
             VMEM((n_hi - 1, rows_dev, 128), F32),
@@ -212,16 +235,16 @@
             dma((count, n_hi - 1)),
         ],
         compiler_params=pltpu.CompilerParams(
-            collective_id=0, has_side_effects=True, vmem_limit_bytes=48 * 1024 * 1024
+            collective_id=0, has_side_effects=True, vmem_limit_bytes=32 * 1024 * 1024
         ),
-    )(part.reshape(n_hi, 2, rows_dev, n), squares.reshape(n_hi, 2, rows_dev, 128))
-
-
-def state_kernel(groups, per_group, head_dim, decay, stride_t, b_all, c_all, prior, updated, readout, left):
-    row = pl.program_id(0)
+    )(residual, gain.reshape(1, width), mix_w, group_w, step_w)
+
+
+def state_kernel(batch, groups, per_group, head_dim, decay, stride_t, b_all, c_all, prior, updated, readout, left):
+    turn = pl.program_id(0)
     rows, state = b_all.shape[0], prior.shape[3]
 
-    @pl.when(row == 0)
+    @pl.when(turn == 0)
     def _():
         wide = stride_t[...]
         high = wide.astype(BF16)
@@ -230,30 +253,32 @@
         left[...] = jnp.where(lane < 2 * rows, high.astype(F32), low.astype(F32)).astype(BF16)
 
     line = lax.broadcasted_iota(jnp.int32, (3 * rows, state), 0)
-    chosen = lax.rem(line, rows) == row
     middle = (line >= rows) & (line < 2 * rows)
-    own_row = lax.broadcasted_iota(jnp.int32, (rows, state), 0) == row
     span = per_group * head_dim
-    for g in range(groups):
-        b = b_all[:, g * state : (g + 1) * state]
-        b = jnp.concatenate([b, b, b], axis=0)
-        b_high = b.astype(BF16).astype(F32)
-        b = jnp.where(chosen, jnp.where(middle, b - b_high, b_high), 0.0).astype(BF16)
-        c = c_all[:, g * state : (g + 1) * state]
-        c = jnp.sum(jnp.where(own_row, c, 0.0), axis=0, keepdims=True)
-        c_high = c.astype(BF16).astype(F32)
-        place = lax.broadcasted_iota(jnp.int32, (16, state), 0)
-        c = jnp.where(place == 0, c_high, jnp.where(place == 1, c - c_high, 0.0)).astype(BF16)
-        outer = jnp.dot(left[g * span : (g + 1) * span, :], b, preferred_element_type=F32)
-        pieces = []
-        for e in range(per_group):
-            h = g * per_group + e
-            value = decay[row, h] * prior[0, h] + outer[e * head_dim : (e + 1) * head_dim]
-            updated[0, h] = value
-            pieces.append(value.astype(BF16))
-        block = jnp.concatenate(pieces, axis=0)
-        found = lax.dot_general(c, block, (((1,), (1,)), ((), ())), preferred_element_type=F32)
-        readout[0, :, g * span : (g + 1) * span] = jnp.sum(found, axis=0, keepdims=True)
+    for i in range(batch):
+        row = turn * batch + i
+        chosen = lax.rem(line, rows) == row
+        own_row = lax.broadcasted_iota(jnp.int32, (rows, state), 0) == row
+        for g in range(groups):
+            b = b_all[:, g * state : (g + 1) * state]
+            b = jnp.concatenate([b, b, b], axis=0)
+            b_high = b.astype(BF16).astype(F32)
+            b = jnp.where(chosen, jnp.where(middle, b - b_high, b_high), 0.0).astype(BF16)
+            c = c_all[:, g * state : (g + 1) * state]
+            c = jnp.sum(jnp.where(own_row, c, 0.0), axis=0, keepdims=True)
+            c_high = c.astype(BF16).astype(F32)
+            place = lax.broadcasted_iota(jnp.int32, (16, state), 0)
+            c = jnp.where(place == 0, c_high, jnp.where(place == 1, c - c_high, 0.0)).astype(BF16)
+            outer = jnp.dot(left[g * span : (g + 1) * span, :], b, preferred_element_type=F32)
+            pieces = []
+            for e in range(per_group):
+                h = g * per_group + e
+                value = decay[row, h] * prior[i, h] + outer[e * head_dim : (e + 1) * head_dim]
+                updated[i, h] = value
+                pieces.append(value.astype(BF16))
+            block = jnp.concatenate(pieces, axis=0)
+            found = lax.dot_general(c, block, (((1,), (1,)), ((), ())), preferred_element_type=F32)
+            readout[i, :, g * span : (g + 1) * span] = jnp.sum(found, axis=0, keepdims=True)
 
 
 def state_step(decay, stride, b_vector, c_vector, prior):
@@ -261,17 +286,18 @@
     groups = b_vector.shape[1] // state
     turned = stride.T
     vmem = pl.BlockSpec(memory_space=VMEM)
-    block = pl.BlockSpec((1, heads, head_dim, state), lambda r: (r, 0, 0, 0))
+    batch = 2 if rows % 2 == 0 else 1
+    block = pl.BlockSpec((batch, heads, head_dim, state), lambda r: (r, 0, 0, 0))
     mix = heads * head_dim
     updated, readout = pl.pallas_call(
-        functools.partial(state_kernel, groups, heads // groups, head_dim),
-        grid=(rows,),
+        functools.partial(state_kernel, batch, groups, heads // groups, head_dim),
+        grid=(rows // batch,),
         out_shape=(
             jax.ShapeDtypeStruct(prior.shape, F32),
             jax.ShapeDtypeStruct((rows, 1, mix), F32),
         ),
         in_specs=[pl.BlockSpec(memory_space=pltpu.SMEM), vmem, vmem, vmem, block],
-        out_specs=(block, pl.BlockSpec((1, 1, mix), lambda r: (r, 0, 0))),
+        out_specs=(block, pl.BlockSpec((batch, 1, mix), lambda r: (r, 0, 0))),
         scratch_shapes=[VMEM((mix, 3 * rows), BF16)],
         compiler_params=pltpu.CompilerParams(vmem_limit_bytes=48 * 1024 * 1024),
         cost_estimate=pl.CostEstimate(flops=4 * prior.size * 48, bytes_accessed=8 * prior.size, transcendentals=0),
@@ -515,19 +541,17 @@
     n_req, n_head = lax.axis_size("req"), lax.axis_size("head")
     width_all = width_dev * n_req
     taps_all = conv_mix.shape[0]
-    wide = residual.astype(F32)
-    squares = jnp.broadcast_to(jnp.sum(wide * wide, axis=1, keepdims=True), (rows, 128))
-    scaled = (wide * norm_first).astype(BF16)
     steps_pad = -heads_dev % 128
-    pieces = [
-        jnp.dot(scaled, mix_weight[:, 0], preferred_element_type=F32),
-        jnp.dot(scaled, mix_weight[:, 1], preferred_element_type=F32),
-        jnp.dot(scaled, group_weight[:, 0], preferred_element_type=F32),
-        jnp.dot(scaled, group_weight[:, 1], preferred_element_type=F32),
-        jnp.pad(jnp.dot(scaled, step_weight, preferred_element_type=F32), ((0, 0), (0, steps_pad))),
-    ]
-    part = jnp.concatenate([piece.astype(BF16) for piece in pieces], axis=1)
-    sums = project(part, squares, n_req, n_head, width_all)
+    sums = project(
+        residual,
+        norm_first,
+        mix_weight.reshape(width_dev, 2 * mix_dev),
+        group_weight.reshape(width_dev, 2 * group_dev),
+        jnp.pad(step_weight, ((0, 0), (0, steps_pad))),
+        n_req,
+        n_head,
+        width_all,
+    )
     gate_z = sums[:, :mix_dev]
     mix_in = sums[:, mix_dev : 2 * mix_dev]
     group_in = sums[:, 2 * mix_dev : 2 * mix_dev + 2 * group_dev].reshape(rows_dev, 2, group_dev)

time: 140 us -> 128 us (0.914)
  matrix products: 4.19 us -> 0 us
  Pallas kernels: 115 us -> 111 us
  local copies, waits for them, and re-layouts: 13.1 us -> 9.8 us
    slice x2 -> x0, local copies, waits for them, and re-layouts: 9.58 us -> none  [the longest x1 8.85 us: on_device(): mix_weight[:, 1]]
    unnamed x27 -> x23, local copies, waits for them, and re-layouts: 0.9 us -> 7.36 us
    dot_general x5 -> x0, matrix products: 4.19 us -> none  [the longest x1 1.37 us: on_device(): jnp.dot(scaled, mix_weight[:, 1], preferred_element_type=F32)]
    pallas_call x1, Pallas kernels: 19.5 us -> 16 us  [state_step(): pl.pallas_call(functools.partial(state_kernel, batch, groups, heads // gr...]
where the time goes in v2:
time: 128 us
  Pallas kernels  111 us (87%)
  local copies, waits for them, and re-layouts  9.8 us (8%)
  other arithmetic  5.43 us (4%)
    pallas_call x1, Pallas kernels, mlp(): pl.pallas_call(functools.partial(mlp_kernel, n_req, n_head, width_all, y_...  68.2 us
    pallas_call x1, Pallas kernels, project(): pl.pallas_call(functools.partial(project_kernel, n_req, n_head, width_all...  27.1 us
    pallas_call x1, Pallas kernels, state_step(): pl.pallas_call(functools.partial(state_kernel, batch, groups, heads // gr...  16 us
    unnamed x23, local copies, waits for them, and re-layouts  7.36 us

profile of v2, /device:TPU:0, one launch (start us, length us, event | category | flops | bytes accessed | tf_op | source)
XLA Modules:
  0.0 127.5 jit_solution(10103216023685573015)
XLA Ops:
  0.7 0.7 exp.22
  1.3 0.7 minimum_subtract_fusion
  2.0 0.7 compare_convert_fusion
  2.7 0.1 copy.35
  2.8 0.7 broadcast_in_dim.8
  3.5 0.1 mul.115
  3.6 1.0 broadcast_multiply_fusion.1
  4.6 0.9 copy.34
  5.5 1.1 broadcast_multiply_fusion
  6.6 1.1 copy.41
  7.7 0.0 copy-start.8
  7.7 0.0 copy-start.5
  7.8 4.6 %copy.40 = bf16[64,8,2,2048]{3,1,2,0:T(8,128)(2,1)S(1)} copy(bf16[64,8,2,2048]{3,2,1,0:T(2,128)(2,1)} %bitcast.26) | data formatting | bytes 8388608
  12.4 0.0 copy-start.3
  12.4 27.1 %shard_map.228 = f32[16,4736]{1,0:T(8,128)S(1)} custom-call(bf16[128,512]{1,0:T(8,128)(2,1)S(1)} %copy-done, f32[1,512]{1,0:T(1,128)S(1)} %bitcast.24, bf16[512,4096]{1,0:T(8,128)(2,1)S(1)} %bitcast.22, bf16[512,512]{1,0:T(8,128)(2,1)S(1)} %bitcast.23, bf16[512,128]{1,0:T(8,128)(2,1)S(1)} %pad.4.step_w), custom_call_target="tpu_custom_call" | custom-call | tf_op jit(solution)/shard_map/pallas_call | solution.py:218
  39.6 0.1 exponential_multiply_fusion
  39.7 0.1 fusion.5
  39.8 0.7 fusion.6
  40.5 0.1 fusion.1
  40.6 0.8 fusion.2
  41.4 0.1 broadcast_in_dim.6
  41.5 0.1 reshape.92
  41.7 0.3 copy.38.stride_t
  42.0 0.0 copy-start.6
  42.1 0.0 copy-start.2
  42.1 16.0 %shard_map.229 = (f32[16,32,64,128]{3,2,1,0:T(8,128)}, f32[16,1,2048]{2,1,0:T(1,128)S(1)}) custom-call(f32[16,32]{1,0:T(8,128)S(1)} %get-tuple-element.10.decay, f32[2048,48]{1,0:T(8,128)S(1)} %copy.38.stride_t, f32[16,256]{1,0:T(8,128)S(1)} %get-tuple-element.13.b_all, f32[16,256]{1,0:T(8,128)S(1)} %get-tuple-element.12.c_all, f32[16,32,64,128]{3,2,1,0:T(8,128)} %prior.1), custom_call_target="tpu_custom_call" | custom-call | flops 805306368 | bytes 33554432 | tf_op jit(solution)/shard_map/pallas_call | solution.py:292
  58.1 0.1 fusion.8
  58.2 0.1 mul.121
  58.3 0.1 reduce_sum.29
  58.4 0.1 mul.122
  58.6 68.2 %shard_map.230 = bf16[128,512]{1,0:T(8,128)(2,1)S(1)} custom-call(bf16[128,512]{1,0:T(8,128)(2,1)S(1)} %copy-done, bf16[16,2048]{1,0:T(8,128)(2,1)S(1)} %multiply_convert_fusion.y_own, f32[1,512]{1,0:T(1,128)S(1)} %bitcast.25, bf16[2048,512]{1,0:T(8,128)(2,1)} %out_w.1, bf16[512,5376]{1,0:T(8,128)(2,1)} %up_w.1, bf16[5376,512]{1,0:T(8,128)(2,1)} %down_w.1), custom_call_target="tpu_custom_call" | custom-call | tf_op jit(solution)/shard_map/pallas_call | solution.py:462
  126.9 0.7 copy.49
  (25 shorter events, 0.3 us)
Async XLA Ops:
  0.6 11.8 %copy-start = (bf16[128,512]{1,0:T(8,128)(2,1)S(1)}, bf16[128,512]{1,0:T(8,128)(2,1)}, u32[]{:S(2)}) copy-start(bf16[128,512]{1,0:T(8,128)(2,1)} %residual.3) | copy-start | bytes 393220
  0.6 11.8 %copy-start.1 = (f32[512]{0:T(512)S(1)}, f32[512]{0:T(512)}, u32[]{:S(2)}) copy-start(f32[512]{0:T(512)} %param.26) | copy-start | bytes 6148
  7.7 31.8 %copy-start.8 = (f32[32]{0:T(128)S(1)}, f32[32]{0:T(128)}, u32[]{:S(2)}) copy-start(f32[32]{0:T(128)} %param.34) | copy-start | bytes 388
  7.7 31.9 %copy-start.5 = (f32[4,2,256]{2,1,0:T(2,128)S(1)}, f32[4,2,256]{2,1,0:T(2,128)}, u32[]{:S(2)}) copy-start(f32[4,2,256]{2,1,0:T(2,128)} %param.31) | copy-start | bytes 24580
  7.7 32.7 %copy-start.7 = (f32[2,256]{1,0:T(2,128)S(1)}, f32[2,256]{1,0:T(2,128)}, u32[]{:S(2)}) copy-start(f32[2,256]{1,0:T(2,128)} %param.33) | copy-start | bytes 6148
  7.8 32.8 %copy-start.4 = (f32[4,2048]{1,0:T(4,128)S(1)}, f32[4,2048]{1,0:T(4,128)}, u32[]{:S(2)}) copy-start(f32[4,2048]{1,0:T(4,128)} %param.30) | copy-start | bytes 98308
  12.4 29.2 %copy-start.3 = (f32[2048]{0:T(1024)S(1)}, f32[2048]{0:T(1024)}, u32[]{:S(2)}) copy-start(f32[2048]{0:T(1024)} %param.32) | copy-start | bytes 24580
  42.0 16.5 %copy-start.6 = (f32[2048]{0:T(1024)S(1)}, f32[2048]{0:T(1024)}, u32[]{:S(2)}) copy-start(f32[2048]{0:T(1024)} %param.37) | copy-start | bytes 24580
  42.1 16.6 %copy-start.2 = (f32[512]{0:T(512)S(1)}, f32[512]{0:T(512)}, u32[]{:S(2)}) copy-start(f32[512]{0:T(512)} %param.39) | copy-start | bytes 6148

commit v3 on v2

--- a/solution.py
+++ b/solution.py
@@ -175,6 +175,10 @@
     norm.send_pair()
     scaled = (wide * gain[...]).astype(BF16)
     mix = mix_w.shape[1]
+    heads = step_w.shape[0]
+    steps = step_w[...]
+    if heads % 128:
+        steps = jnp.concatenate([steps, jnp.zeros((-heads % 128, steps.shape[1]), BF16)], axis=0)
     moves = []
     for c, (s, w) in enumerate(chunks):
         if s < mix:
@@ -183,7 +187,7 @@
             product = jnp.concatenate(
                 [
                     jnp.dot(scaled, group_w[...], preferred_element_type=F32),
-                    jnp.dot(scaled, step_w[...], preferred_element_type=F32),
+                    lax.dot_general(scaled, steps, (((1,), (1,)), ((), ())), preferred_element_type=F32),
                 ],
                 axis=1,
             )
@@ -207,11 +211,11 @@
 
 def project(residual, gain, mix_w, group_w, step_w, n_req, n_head, width_all):
     rows, width = residual.shape
-    mix, rest = mix_w.shape[1], group_w.shape[1] + step_w.shape[1]
+    mix, rest = mix_w.shape[1], group_w.shape[1] + -(-step_w.shape[0] // 128) * 128
     n = mix + rest
     rows_dev = rows // n_req
     n_hi = n_req // 2
-    chunks = spans(mix, 1024) + [(mix, rest)]
+    chunks = spans(mix, 512) + [(mix, rest)]
     count = len(chunks) + 1
     dma = pltpu.SemaphoreType.DMA
     vmem = pl.BlockSpec(memory_space=VMEM)
@@ -240,7 +244,7 @@
     )(residual, gain.reshape(1, width), mix_w, group_w, step_w)
 
 
-def state_kernel(batch, groups, per_group, head_dim, decay, stride_t, b_all, c_all, prior, updated, readout, left):
+def state_kernel(batch, groups, per_group, head_dim, lengths, decay, stride_t, b_all, c_all, prior, updated, readout, left):
     turn = pl.program_id(0)
     rows, state = b_all.shape[0], prior.shape[3]
 
@@ -258,6 +262,7 @@
     for i in range(batch):
         row = turn * batch + i
         chosen = lax.rem(line, rows) == row
+        alive = jnp.where(lengths[row] > 0, 1.0, 0.0)
         own_row = lax.broadcasted_iota(jnp.int32, (rows, state), 0) == row
         for g in range(groups):
             b = b_all[:, g * state : (g + 1) * state]
@@ -273,7 +278,7 @@
             pieces = []
             for e in range(per_group):
                 h = g * per_group + e
-                value = decay[row, h] * prior[i, h] + outer[e * head_dim : (e + 1) * head_dim]
+                value = (decay[row, h] * alive) * prior[i, h] + outer[e * head_dim : (e + 1) * head_dim]
                 updated[i, h] = value
                 pieces.append(value.astype(BF16))
             block = jnp.concatenate(pieces, axis=0)
@@ -281,7 +286,7 @@
             readout[i, :, g * span : (g + 1) * span] = jnp.sum(found, axis=0, keepdims=True)
 
 
-def state_step(decay, stride, b_vector, c_vector, prior):
+def state_step(lengths, decay, stride, b_vector, c_vector, prior):
     rows, heads, head_dim, state = prior.shape
     groups = b_vector.shape[1] // state
     turned = stride.T
@@ -296,12 +301,12 @@
             jax.ShapeDtypeStruct(prior.shape, F32),
             jax.ShapeDtypeStruct((rows, 1, mix), F32),
         ),
-        in_specs=[pl.BlockSpec(memory_space=pltpu.SMEM), vmem, vmem, vmem, block],
+        in_specs=[pl.BlockSpec(memory_space=pltpu.SMEM)] * 2 + [vmem, vmem, vmem, block],
         out_specs=(block, pl.BlockSpec((batch, 1, mix), lambda r: (r, 0, 0))),
         scratch_shapes=[VMEM((mix, 3 * rows), BF16)],
         compiler_params=pltpu.CompilerParams(vmem_limit_bytes=48 * 1024 * 1024),
         cost_estimate=pl.CostEstimate(flops=4 * prior.size * 48, bytes_accessed=8 * prior.size, transcendentals=0),
-    )(decay, jnp.concatenate([turned, turned, turned], axis=1), b_vector, c_vector, prior)
+    )(lengths, decay, jnp.concatenate([turned, turned, turned], axis=1), b_vector, c_vector, prior)
     return updated, readout.reshape(rows, mix)
 
 
@@ -451,8 +456,8 @@
     rows_dev, mix = y_own.shape
     ff = up_w.shape[1]
     n_hi = n_req // 2
-    y_chunks = spans(mix, 1024)
-    chunks = spans(ff, 896)
+    y_chunks = spans(mix, 512)
+    chunks = spans(ff, 512)
     count, y_count = len(chunks), len(y_chunks)
     rows_head = rows // n_head
     dma = pltpu.SemaphoreType.DMA
@@ -541,13 +546,12 @@
     n_req, n_head = lax.axis_size("req"), lax.axis_size("head")
     width_all = width_dev * n_req
     taps_all = conv_mix.shape[0]
-    steps_pad = -heads_dev % 128
     sums = project(
         residual,
         norm_first,
         mix_weight.reshape(width_dev, 2 * mix_dev),
         group_weight.reshape(width_dev, 2 * group_dev),
-        jnp.pad(step_weight, ((0, 0), (0, steps_pad))),
+        step_weight.T,
         n_req,
         n_head,
         width_all,
@@ -556,19 +560,19 @@
     mix_in = sums[:, mix_dev : 2 * mix_dev]
     group_in = sums[:, 2 * mix_dev : 2 * mix_dev + 2 * group_dev].reshape(rows_dev, 2, group_dev)
     step_raw = sums[:, 2 * mix_dev + 2 * group_dev : 2 * mix_dev + 2 * group_dev + heads_dev]
-    valid = jnp.minimum(lengths, taps_all - 1)
     slots = jnp.arange(taps_all - 1)
-    keep = (slots[None, :] >= (taps_all - 1 - valid)[:, None]).astype(F32)
+    keep = (slots[None, :] + lengths[:, None] >= taps_all - 1).astype(F32)
     window_mix = jnp.concatenate([tail_mix * keep[:, :, None], mix_in[:, None, :]], axis=1)
     window_group = jnp.concatenate([tail_group * keep[:, :, None, None], group_in[:, None]], axis=1)
     conv_x = jax.nn.silu(jnp.sum(window_mix * conv_mix[None], axis=1) + bias_mix)
     conv_bc = jax.nn.silu(jnp.sum(window_group * conv_group[None], axis=1) + bias_group)
     step_size = jax.nn.softplus(step_raw + step_bias)
-    alive = (lengths > 0).astype(F32)
-    decay = jnp.exp(-step_size * jnp.exp(decay_log)) * alive[:, None]
-    stride = jnp.repeat(step_size, head_dim, axis=1) * conv_x
-    state_out, readout = state_step(decay, stride, conv_bc[:, 0], conv_bc[:, 1], ssm_state)
-    mixed = readout + jnp.repeat(skip_gain, head_dim)[None, :] * conv_x
+    decay = jnp.exp(-step_size * jnp.exp(decay_log))
+    gains = jnp.broadcast_to(skip_gain[None, :], step_size.shape)
+    repeated = jnp.repeat(jnp.concatenate([step_size, gains], axis=0), head_dim, axis=1)
+    stride = repeated[:rows_dev] * conv_x
+    state_out, readout = state_step(lengths, decay, stride, conv_bc[:, 0], conv_bc[:, 1], ssm_state)
+    mixed = readout + repeated[rows_dev:] * conv_x
     gated = mixed * jax.nn.silu(gate_z)
     grouped = gated.reshape(rows_dev, groups_dev, -1)
     inverse = lax.rsqrt(jnp.mean(grouped * grouped, axis=2, keepdims=True) + eps)

time: 128 us -> 137 us (1.070)
  Pallas kernels: 111 us -> 123 us
    pallas_call x1, Pallas kernels: 68.2 us -> 76.2 us  [mlp(): pl.pallas_call(functools.partial(mlp_kernel, n_req, n_head, width_all, y_...]
    pallas_call x1, Pallas kernels: 27.1 us -> 30.3 us  [project(): pl.pallas_call(functools.partial(project_kernel, n_req, n_head, width_all...]
    unnamed x23 -> x26, local copies, waits for them, and re-layouts: 7.36 us -> 6.49 us
where the time goes in v3:
time: 137 us
  Pallas kernels  123 us (90%)
  local copies, waits for them, and re-layouts  8.9 us (6%)
  other arithmetic  4.72 us (3%)
    pallas_call x1, Pallas kernels, mlp(): pl.pallas_call(functools.partial(mlp_kernel, n_req, n_head, width_all, y_...  76.2 us
    pallas_call x1, Pallas kernels, project(): pl.pallas_call(functools.partial(project_kernel, n_req, n_head, width_all...  30.3 us
    pallas_call x1, Pallas kernels, state_step(): pl.pallas_call(functools.partial(state_kernel, batch, groups, heads // gr...  16 us
    unnamed x26, local copies, waits for them, and re-layouts  6.49 us

profile of v3, /device:TPU:0, one launch (start us, length us, event | category | flops | bytes accessed | tf_op | source)
XLA Modules:
  0.0 137.1 jit_solution(8611796587216047256)
XLA Ops:
  0.7 0.7 exp.22
  1.4 0.7 fusion.7
  2.0 0.1 copy.32
  2.1 0.7 broadcast_in_dim.12
  2.8 0.1 broadcast_in_dim.13
  2.9 1.0 broadcast_multiply_fusion.1
  3.9 1.1 broadcast_multiply_fusion
  5.0 1.1 copy.38
  6.2 0.0 copy-start.10
  6.2 0.0 copy-start.7
  6.2 0.0 copy-start.9
  6.2 0.0 copy-start.6
  6.2 4.6 %copy.37 = bf16[64,8,2,2048]{3,1,2,0:T(8,128)(2,1)S(1)} copy(bf16[64,8,2,2048]{3,2,1,0:T(2,128)(2,1)} %bitcast.28) | data formatting | bytes 8388608
  10.8 0.0 copy-start.5
  10.8 0.0 copy-start.2
  10.9 30.3 %shard_map.228 = f32[16,4736]{1,0:T(8,128)S(1)} custom-call(bf16[128,512]{1,0:T(8,128)(2,1)S(1)} %copy-done, f32[1,512]{1,0:T(1,128)S(1)} %bitcast.26, bf16[512,4096]{1,0:T(8,128)(2,1)S(1)} %bitcast.23, bf16[512,512]{1,0:T(8,128)(2,1)S(1)} %bitcast.24, bf16[32,512]{1,0:T(8,128)(2,1)S(1)} %bitcast.25), custom_call_target="tpu_custom_call" | custom-call | tf_op jit(solution)/shard_map/pallas_call | solution.py:222
  41.3 0.1 fusion.5
  41.4 0.7 fusion.6
  42.1 0.1 fusion.1
  42.2 0.8 fusion.2
  43.0 0.1 broadcast_in_dim.10
  43.1 0.1 slice.33
  43.3 0.3 copy.35.stride_t
  43.7 0.0 copy-start.8
  43.7 0.0 copy-start.4
  43.7 16.0 %shard_map.229 = (f32[16,32,64,128]{3,2,1,0:T(8,128)}, f32[16,1,2048]{2,1,0:T(1,128)S(1)}) custom-call(s32[16]{0:T(128)S(1)} %copy-done.2, f32[16,32]{1,0:T(8,128)S(1)} %get-tuple-element.10.decay, f32[2048,48]{1,0:T(8,128)S(1)} %copy.35.stride_t, f32[16,256]{1,0:T(8,128)S(1)} %get-tuple-element.13.b_all, f32[16,256]{1,0:T(8,128)S(1)} %get-tuple-element.12.c_all, ...), custom_call_target="tpu_custom_call" | custom-call | flops 805306368 | bytes 33554432 | tf_op jit(solution)/shard_map/pallas_call | solution.py:297
  59.7 0.1 fusion.8
  59.8 0.1 mul.102
  59.9 0.1 reduce_sum.29
  60.1 0.1 mul.103
  60.3 76.2 %shard_map.230 = bf16[128,512]{1,0:T(8,128)(2,1)S(1)} custom-call(bf16[128,512]{1,0:T(8,128)(2,1)S(1)} %copy-done, bf16[16,2048]{1,0:T(8,128)(2,1)S(1)} %multiply_convert_fusion.y_own, f32[1,512]{1,0:T(1,128)S(1)} %bitcast.27, bf16[2048,512]{1,0:T(8,128)(2,1)} %out_w.1, bf16[512,5376]{1,0:T(8,128)(2,1)} %up_w.1, bf16[5376,512]{1,0:T(8,128)(2,1)} %down_w.1), custom_call_target="tpu_custom_call" | custom-call | tf_op jit(solution)/shard_map/pallas_call | solution.py:467
  136.4 0.7 copy.46
  (25 shorter events, 0.3 us)
Async XLA Ops:
  0.6 10.2 %copy-start = (bf16[128,512]{1,0:T(8,128)(2,1)S(1)}, bf16[128,512]{1,0:T(8,128)(2,1)}, u32[]{:S(2)}) copy-start(bf16[128,512]{1,0:T(8,128)(2,1)} %residual.3) | copy-start | bytes 393220
  0.6 10.2 %copy-start.1 = (bf16[512,32]{0,1:T(8,128)(2,1)S(1)}, bf16[512,32]{0,1:T(8,128)(2,1)}, u32[]{:S(2)}) copy-start(bf16[512,32]{0,1:T(8,128)(2,1)} %param.29) | copy-start | bytes 98308
  0.7 10.2 %copy-start.3 = (f32[512]{0:T(512)S(1)}, f32[512]{0:T(512)}, u32[]{:S(2)}) copy-start(f32[512]{0:T(512)} %param.26) | copy-start | bytes 6148
  6.2 35.1 %copy-start.10 = (f32[32]{0:T(128)S(1)}, f32[32]{0:T(128)}, u32[]{:S(2)}) copy-start(f32[32]{0:T(128)} %param.34) | copy-start | bytes 388
  6.2 35.1 %copy-start.7 = (f32[4,2,256]{2,1,0:T(2,128)S(1)}, f32[4,2,256]{2,1,0:T(2,128)}, u32[]{:S(2)}) copy-start(f32[4,2,256]{2,1,0:T(2,128)} %param.31) | copy-start | bytes 24580
  6.2 35.9 %copy-start.9 = (f32[2,256]{1,0:T(2,128)S(1)}, f32[2,256]{1,0:T(2,128)}, u32[]{:S(2)}) copy-start(f32[2,256]{1,0:T(2,128)} %param.33) | copy-start | bytes 6148
  6.2 35.9 %copy-start.6 = (f32[4,2048]{1,0:T(4,128)S(1)}, f32[4,2048]{1,0:T(4,128)}, u32[]{:S(2)}) copy-start(f32[4,2048]{1,0:T(4,128)} %param.30) | copy-start | bytes 98308
  10.8 32.4 %copy-start.5 = (f32[2048]{0:T(1024)S(1)}, f32[2048]{0:T(1024)}, u32[]{:S(2)}) copy-start(f32[2048]{0:T(1024)} %param.32) | copy-start | bytes 24580
  10.8 32.8 %copy-start.2 = (s32[16]{0:T(128)S(1)}, s32[16]{0:T(128)}, u32[]{:S(2)}) copy-start(s32[16]{0:T(128)} %lengths.1) | copy-start | bytes 196
  43.7 16.5 %copy-start.8 = (f32[2048]{0:T(1024)S(1)}, f32[2048]{0:T(1024)}, u32[]{:S(2)}) copy-start(f32[2048]{0:T(1024)} %param.37) | copy-start | bytes 24580
  43.7 16.6 %copy-start.4 = (f32[512]{0:T(512)S(1)}, f32[512]{0:T(512)}, u32[]{:S(2)}) copy-start(f32[512]{0:T(512)} %param.39) | copy-start | bytes 6148
